TPU v7x, 32 devices: a whole 2x2x4 slice. The times are simulated.
32 devices in a mesh: groups: 2 (over x), gx: 16 (over z, y, core).
Axes of the slice: x: 2, y: 2, z: 4, core: 2. Of those that a mesh axis runs over, the one named last changes fastest.
Arguments:
- right_side: float32 [256, 256, 512], P(('groups', 'gx')), parts along dimension 0, may hold values from -14 to 14
- kappa_sq: float32 [256, 256, 512], P(('groups', 'gx')), parts along dimension 0, may hold values from 0.1 to 4
- depth: int32 [256, 256], P(('groups', 'gx')), parts along dimension 0, may hold values from 128 to 512
- agg_ids: int32 [1024], P(('groups', 'gx')), parts along dimension 0, may hold values from 0 to 255, as said below
- coarse_inverse: float32 [512, 256], P('groups'), parts along dimension 0, may hold values from -3 to 3
Outputs:
- applied: float32 [256, 256, 512], P(('groups', 'gx')), parts along dimension 0
There are 2 independent parts, one for each index of `groups`. A program takes and returns all parts, laid end to end along the dimension named above; each array names one. Nothing has to cross between parts.
Inputs may be any that keep to these rules, and one draw needn't show every extreme that they name: `agg_ids`: each aggregate 0 to 255 is named by exactly two coarse blocks.
All inputs are finite; a program needn't handle non-finite values.
Results may differ from a plain program's by a relative error of at most 0.0003.
Values sent between devices are 32-bit elements; how exact they have to be, the bound alone decides.
A program may use at most 128 MiB of HBM per device.

v0:
```python
import jax
import jax.numpy as jnp
from jax import lax
from jax.sharding import PartitionSpec as P

MARGIN = 4
SWEEPS = 4
BY = 64
BZ = 64
BLOCK_CELLS = 32768


def extended(cells, sides, width):
    for axis, dim in sides:
        count = lax.axis_size(axis)
        ends = count - 1
        head = lax.slice_in_dim(cells, 0, width, axis=dim)
        tail = lax.slice_in_dim(cells, cells.shape[dim] - width, cells.shape[dim], axis=dim)
        cells = jnp.concatenate(
            [
                lax.ppermute(tail, axis, [(i, (i + 1) % count) for i in range(ends)]),
                cells,
                lax.ppermute(head, axis, [((i + 1) % count, i) for i in range(ends)]),
            ],
            axis=dim,
        )
    return cells


def from_behind(value, axis, steps):
    count = lax.axis_size(axis)
    first, last = (max(0, -steps), min(count, count - steps))
    return lax.ppermute(value, axis, [(source, source + steps) for source in range(first, last)])


def neighbour_sum(u):
    padded = jnp.pad(u, 1)
    total = 4.0 * (padded[2:, 1:-1, 1:-1] + padded[:-2, 1:-1, 1:-1])
    total = total + padded[1:-1, 2:, 1:-1] + padded[1:-1, :-2, 1:-1]
    total = total + padded[1:-1, 1:-1, 2:] + padded[1:-1, 1:-1, :-2]
    return total


def on_device(right_side, kappa_sq, depth, agg_ids, coarse_inverse):
    slab, width_y, width_z = right_side.shape
    depth_idx = lax.broadcasted_iota(jnp.int32, right_side.shape, 2)
    mask = (depth_idx < depth[:, :, None]).astype(jnp.float32)
    dinv = mask / (kappa_sq + 12.0)
    masked = mask * right_side
    block_sums = (
        masked.reshape(slab, width_y // BY, BY, width_z // BZ, BZ).sum(axis=(0, 2, 4)).reshape(-1)
        / BLOCK_CELLS
    )
    count = coarse_inverse.shape[0]
    onehot = (agg_ids[:, None] == jnp.arange(count, dtype=jnp.int32)[None, :]).astype(jnp.float32)
    partial_rhs = jnp.dot(block_sums, onehot, precision=lax.Precision.HIGHEST)
    coarse_rhs = lax.psum(partial_rhs, "gx")
    ext = extended(dinv, (("gx", 0),), MARGIN)
    local_mask = (ext > 0).astype(jnp.float32)
    source = jnp.pad(masked, ((MARGIN, MARGIN), (0, 0), (0, 0)))
    field = source
    for sweep in range(SWEEPS):
        field = source + local_mask * neighbour_sum(ext * field)
    solved = ext * field
    lower_rim = solved[:MARGIN]
    upper_rim = solved[MARGIN + slab :]
    middle = solved[MARGIN : MARGIN + slab]
    from_left = from_behind(upper_rim, "gx", 1)
    from_right = from_behind(lower_rim, "gx", -1)
    fine = middle + jnp.pad(from_left, ((0, slab - MARGIN), (0, 0), (0, 0)))
    fine = fine + jnp.pad(from_right, ((slab - MARGIN, 0), (0, 0), (0, 0)))
    coarse_sol = jnp.dot(coarse_inverse, coarse_rhs, precision=lax.Precision.HIGHEST)
    per_block = jnp.dot(onehot, coarse_sol, precision=lax.Precision.HIGHEST)
    per_block = per_block.reshape(1, width_y // BY, 1, width_z // BZ, 1)
    coarse = jnp.broadcast_to(per_block, (slab, width_y // BY, BY, width_z // BZ, BZ)).reshape(
        slab, width_y, width_z
    )
    return fine + mask * coarse


def solution(mesh):
    in_specs = (
        P(("groups", "gx"), None, None),
        P(("groups", "gx"), None, None),
        P(("groups", "gx"), None),
        P(("groups", "gx")),
        P("groups", None),
    )
    out_specs = P(("groups", "gx"), None, None)
    return jax.shard_map(
        on_device, mesh=mesh, in_specs=in_specs, out_specs=out_specs, check_vma=False
    )
```

profile of v0, /device:TPU:9, one launch (start us, length us, event | category | flops | bytes accessed | tf_op | source)
XLA Modules:
  0.0 242.5 jit_solution(3235908514545435231)
XLA Ops:
  0.0 0.0 copy-start
  0.0 4.2 %fusion.38 = (f32[256,512]{1,0:T(8,128)S(1)}, f32[8,256,512]{2,1,0:T(8,128)S(1)}, f32[8,256,512]{2,1,0:T(8,128)S(1)}) fusion(f32[8,256,512]{2,1,0:T(8,128)} %param.5, s32[8,256]{1,0:T(8,128)} %param.7, f32[8,256,512]{2,1,0:T(8,128)} %param.6), kind=kLoop, calls=%fused_computation.76 | loop fusion | flops 6160384 | bytes 17309696 | tf_op jit(solution)/shard_map/reduce_sum | solution.py:51
  4.2 0.0 copy-start.1
  4.2 0.0 copy-start.2
  4.2 0.5 fusion.41
  4.7 3.7 %collective-permute-start = (f32[4,256,512]{2,1,0:T(8,128)S(1)}, f32[4,256,512]{2,1,0:T(8,128)S(1)}, u32[]{:S(2)}, u32[]{:S(2)}) collective-permute-start(f32[4,256,512]{2,1,0:T(8,128)S(1)} %get-tuple-element.9), channel_id=1, source_target_pairs={{0,1},{1,2},{2,3},{3,4},{4,5},{5,6},{6,7},{7,8},{8,9},{9,10},{10,1... | collective-permute-start | bytes 6291464 | tf_op jit(solution)/shard_map/ppermute | solution.py:21
  8.4 1.9 collective-permute-start.1
  10.3 43.5 %collective-permute-done = f32[4,256,512]{2,1,0:T(8,128)S(1)} collective-permute-done((f32[4,256,512]{2,1,0:T(8,128)S(1)}, f32[4,256,512]{2,1,0:T(8,128)S(1)}, u32[]{:S(2)}, u32[]{:S(2)}) %collective-permute-start) | collective-permute-done | bytes 2097184 | tf_op jit(solution)/shard_map/ppermute | solution.py:21
  53.8 1.6 collective-permute-done.1
  55.4 0.0 copy-start.3
  55.4 0.0 copy-done.1
  55.4 0.0 copy-done.2
  55.4 1.3 copy-done.3
  56.7 4.2 %pad_multiply_fusion = f32[16,256,512]{2,1,0:T(8,128)} fusion(f32[8,256,512]{2,1,0:T(8,128)S(1)} %get-tuple-element.6, f32[4,256,512]{2,1,0:T(8,128)S(1)} %collective-permute-done.1, f32[8,256,512]{2,1,0:T(8,128)S(1)} %get-tuple-element.11, f32[4,256,512]{2,1,0:T(8,128)S(1)} %collective-permute-done), kind=kLoop, calls=%fused_computation.28 | loop fusion | flops 6291456 | bytes 20971520 | tf_op jit(solution)/shard_map/mul | solution.py:63
  61.0 26.6 %fusion = f32[16,256,512]{2,1,0:T(8,128)} fusion(f32[8,256,512]{2,1,0:T(8,128)} %copy-done.2, f32[16,256,512]{2,1,0:T(8,128)} %pad_multiply_fusion, f32[4,256,512]{2,1,0:T(8,128)} %copy-done.3, f32[8,256,512]{2,1,0:T(8,128)} %copy-done.1, f32[4,256,512]{2,1,0:T(8,128)S(1)} %collective-permute-done), kind=kLoop, calls=%fused_computation.29 | loop fusion | flops 25165824 | bytes 29360128 | tf_op jit(solution)/shard_map/mul | solution.py:63
  87.6 25.7 %fusion.1 = f32[16,256,512]{2,1,0:T(8,128)} fusion(f32[8,256,512]{2,1,0:T(8,128)} %copy-done.2, f32[16,256,512]{2,1,0:T(8,128)} %fusion, f32[4,256,512]{2,1,0:T(8,128)} %copy-done.3, f32[8,256,512]{2,1,0:T(8,128)} %copy-done.1, f32[4,256,512]{2,1,0:T(8,128)S(1)} %collective-permute-done), kind=kLoop, calls=%fused_computation.30 | loop fusion | flops 25165824 | bytes 29360128 | tf_op jit(solution)/shard_map/mul | solution.py:63
  113.3 26.5 %fusion.2 = f32[16,256,512]{2,1,0:T(8,128)} fusion(f32[8,256,512]{2,1,0:T(8,128)} %copy-done.2, f32[16,256,512]{2,1,0:T(8,128)} %fusion.1, f32[4,256,512]{2,1,0:T(8,128)} %copy-done.3, f32[8,256,512]{2,1,0:T(8,128)} %copy-done.1, f32[4,256,512]{2,1,0:T(8,128)S(1)} %collective-permute-done), kind=kLoop, calls=%fused_computation.31 | loop fusion | flops 25165824 | bytes 29360128 | tf_op jit(solution)/shard_map/mul | solution.py:63
  139.8 26.6 %fusion.3 = f32[16,256,512]{2,1,0:T(8,128)} fusion(f32[8,256,512]{2,1,0:T(8,128)} %copy-done.2, f32[16,256,512]{2,1,0:T(8,128)} %fusion.2, f32[4,256,512]{2,1,0:T(8,128)} %copy-done.3, f32[8,256,512]{2,1,0:T(8,128)} %copy-done.1, f32[4,256,512]{2,1,0:T(8,128)S(1)} %collective-permute-done), kind=kLoop, calls=%fused_computation.32 | loop fusion | flops 25165824 | bytes 29360128 | tf_op jit(solution)/shard_map/mul | solution.py:64
  166.4 0.0 copy-start.5
  166.4 0.0 copy-start.4
  166.4 4.7 %fusion.40 = (f32[4,256,512]{2,1,0:T(8,128)}, f32[4,256,512]{2,1,0:T(8,128)}) fusion(f32[16,256,512]{2,1,0:T(8,128)} %fusion.3), kind=kLoop, calls=%fused_computation.77 | loop fusion | bytes 8388608 | tf_op jit(solution)/shard_map/slice | solution.py:66
  171.1 2.8 %collective-permute-start.2 = (f32[4,256,512]{2,1,0:T(8,128)}, f32[4,256,512]{2,1,0:T(8,128)}, u32[]{:S(2)}, u32[]{:S(2)}) collective-permute-start(f32[4,256,512]{2,1,0:T(8,128)} %get-tuple-element.7), channel_id=1, source_target_pairs={{0,1},{1,2},{2,3},{3,4},{4,5},{5,6},{6,7},{7,8},{8,9},{9,10},{10,1... | collective-permute-start | bytes 6291464 | tf_op jit(solution)/shard_map/ppermute | solution.py:33
  174.0 1.9 collective-permute-start.3
  175.9 0.2 reduce_sum.14
  176.1 0.2 reduce_sum.18
  176.3 0.1 reshape.11
  176.4 0.0 copy-done.5
  176.4 0.2 fusion.35
  176.6 59.7 %psum.7 = f32[256]{0:T(256)S(1)} all-reduce(f32[256]{0:T(256)S(1)} %bitcast.14), channel_id=1, replica_groups=mesh['groups'=2,'gx'=16] {'gx'}, use_global_device_ids=true, to_apply=%region_2.3 | all-reduce | flops 256 | bytes 2048 | tf_op jit(solution)/shard_map/psum | solution.py:57
  236.3 0.0 copy-done
  236.3 0.3 convolution_bitcast_fusion
  236.5 0.2 convolution_bitcast_fusion.1
  236.8 0.1 broadcast_in_dim.14
  236.9 0.2 broadcast_in_dim.15
  237.0 0.3 broadcast_in_dim.16
  237.3 0.0 collective-permute-done.2
  237.3 0.0 collective-permute-done.3
  237.3 0.0 copy-done.4
  237.4 5.1 %fusion.33 = f32[8,256,512]{2,1,0:T(8,128)} fusion(f32[16,256,512]{2,1,0:T(8,128)} %fusion.3, f32[4,256,512]{2,1,0:T(8,128)} %collective-permute-done.3, f32[4,256,512]{2,1,0:T(8,128)} %collective-permute-done.2, f32[256,512]{1,0:T(8,128)S(1)} %broadcast_in_dim.16, s32[8,256]{1,0:T(8,128)S(1)} %copy-done.4), kind=kLoop, calls=%fused_computation.64 | loop fusion | flops 5242880 | bytes 13115392 | tf_op jit(solution)/shard_map/add | solution.py:78
  (1 shorter events, 0.0 us)
Async XLA Ops:
  0.0 236.3 %copy-start = (f32[256,256]{1,0:T(8,128)S(1)}, f32[256,256]{1,0:T(8,128)}, u32[]{:S(2)}) copy-start(f32[256,256]{1,0:T(8,128)} %param.9) | copy-start | bytes 786436
  4.2 51.2 %copy-start.1 = (f32[8,256,512]{2,1,0:T(8,128)}, f32[8,256,512]{2,1,0:T(8,128)S(1)}, u32[]{:S(2)}) copy-start(f32[8,256,512]{2,1,0:T(8,128)S(1)} %get-tuple-element.11) | copy-start | bytes 12582916
  4.2 51.2 %copy-start.2 = (f32[8,256,512]{2,1,0:T(8,128)}, f32[8,256,512]{2,1,0:T(8,128)S(1)}, u32[]{:S(2)}) copy-start(f32[8,256,512]{2,1,0:T(8,128)S(1)} %get-tuple-element.6) | copy-start | bytes 12582916
  4.7 49.1 %collective-permute-start = (f32[4,256,512]{2,1,0:T(8,128)S(1)}, f32[4,256,512]{2,1,0:T(8,128)S(1)}, u32[]{:S(2)}, u32[]{:S(2)}) collective-permute-start(f32[4,256,512]{2,1,0:T(8,128)S(1)} %get-tuple-element.9), channel_id=1, source_target_pairs={{0,1},{1,2},{2,3},{3,4},{4,5},{5,6},{6,7},{7,8},{8,9},{9,10},{10,1... | collective-permute-start | bytes 6291464 | tf_op jit(solution)/shard_map/ppermute | solution.py:21
  8.4 47.0 %collective-permute-start.1 = (f32[4,256,512]{2,1,0:T(8,128)S(1)}, f32[4,256,512]{2,1,0:T(8,128)S(1)}, u32[]{:S(2)}, u32[]{:S(2)}) collective-permute-start(f32[4,256,512]{2,1,0:T(8,128)S(1)} %get-tuple-element.10), channel_id=1, source_target_pairs={{1,0},{2,1},{3,2},{4,3},{5,4},{6,5},{7,6},{8,7},{9,8},{10,9},{11,1... | collective-permute-start | bytes 6291464 | tf_op jit(solution)/shard_map/ppermute | solution.py:23
  55.4 1.3 copy-start.3
  166.4 9.9 %copy-start.5 = (s32[32]{0:T(128)S(1)}, s32[32]{0:T(128)}, u32[]{:S(2)}) copy-start(s32[32]{0:T(128)} %param.8) | copy-start | bytes 388
  166.4 70.9 %copy-start.4 = (s32[8,256]{1,0:T(8,128)S(1)}, s32[8,256]{1,0:T(8,128)}, u32[]{:S(2)}) copy-start(s32[8,256]{1,0:T(8,128)} %param.7) | copy-start | bytes 24580
  171.1 66.2 %collective-permute-start.2 = (f32[4,256,512]{2,1,0:T(8,128)}, f32[4,256,512]{2,1,0:T(8,128)}, u32[]{:S(2)}, u32[]{:S(2)}) collective-permute-start(f32[4,256,512]{2,1,0:T(8,128)} %get-tuple-element.7), channel_id=1, source_target_pairs={{0,1},{1,2},{2,3},{3,4},{4,5},{5,6},{6,7},{7,8},{8,9},{9,10},{10,1... | collective-permute-start | bytes 6291464 | tf_op jit(solution)/shard_map/ppermute | solution.py:33
  174.0 63.4 %collective-permute-start.3 = (f32[4,256,512]{2,1,0:T(8,128)}, f32[4,256,512]{2,1,0:T(8,128)}, u32[]{:S(2)}, u32[]{:S(2)}) collective-permute-start(f32[4,256,512]{2,1,0:T(8,128)} %get-tuple-element.8), channel_id=1, source_target_pairs={{1,0},{2,1},{3,2},{4,3},{5,4},{6,5},{7,6},{8,7},{9,8},{10,9},{11,1... | collective-permute-start | bytes 6291464 | tf_op jit(solution)/shard_map/ppermute | solution.py:33
where the time goes:
time: 247 us; the launch traced here: 242 us
  other arithmetic  119 us (48%)
  blocking collectives  59.7 us (24%)
  waiting for transfers between devices  45.1 us (18%)
  starting transfers between devices  10.4 us (4%)
  local copies, waits for them, and re-layouts  7.31 us (3%)
    mul x4, other arithmetic, on_device(): field = source + local_mask * neighbour_sum(ext * field)  83.1 us
    psum x1, blocking collectives, on_device(): coarse_rhs = lax.psum(partial_rhs, 'gx')  59.7 us
    ppermute x1, waiting for transfers between devices, extended(): lax.ppermute(tail, axis, [(i, (i + 1) % count) for i in range(ends)])  43.5 us
    mul x1, other arithmetic, on_device(): solved = ext * field  26.6 us
    add x1, other arithmetic, on_device(): return fine + mask * coarse  5.11 us
  transfers between devices with their start and end apart: 4, of which 2 were waited for; matrix products, arithmetic and copies ran while one was open for 1% of the time, Pallas kernels for 0%

commit v1 on v0

v1 whole, which is shorter than its diff:
```python
import functools

import jax
import jax.numpy as jnp
from jax import lax
from jax.experimental import pallas as pl
from jax.experimental.pallas import tpu as pltpu
from jax.sharding import PartitionSpec as P

SWEEPS = 4
BY = 64
BZ = 64
BLOCK_CELLS = 32768
ROWS = 16
PAD = 8
LANES = 128
CHUNKS = 2
MESH = pl.DeviceIdType.MESH
HIGHEST = lax.Precision.HIGHEST


def in_plane(u, planes_at, y, first, last):
    block = u[planes_at + (pl.ds(y, ROWS + 2 * PAD), slice(None))]
    height, width = block.shape
    up = pltpu.roll(block, 1, 0)[PAD : PAD + ROWS]
    down = pltpu.roll(block, height - 1, 0)[PAD : PAD + ROWS]
    mid = block[PAD : PAD + ROWS]
    count = width // LANES
    cols = [mid[:, i * LANES : (i + 1) * LANES] for i in range(count)]
    right = [pltpu.roll(c, 1, 1) for c in cols]
    left = [pltpu.roll(c, LANES - 1, 1) for c in cols]
    zero = jnp.zeros_like(cols[0])
    below = jnp.concatenate(
        [jnp.where(first, right[i - 1] if i else zero, right[i]) for i in range(count)], axis=1
    )
    above = jnp.concatenate(
        [jnp.where(last, left[i + 1] if i + 1 < count else zero, left[i]) for i in range(count)],
        axis=1,
    )
    return (up + down) + (below + above)


def kernel(
    n, right_ref, kappa_ref, depth_ref, agg_ref, inverse_ref, out_ref,
    u, dinv, data, part, parts, in_sem, send_sem, recv_sem, part_send, part_recv, out_sem,
):
    slab, ny, nz = right_ref.shape
    me = lax.axis_index("gx")
    order = [p for pair in zip(range(slab // 2), range(slab - 1, slab // 2 - 1, -1)) for p in pair]
    loads = {}
    for p in order:
        loads[p] = [
            pltpu.make_async_copy(right_ref.at[p], data.at[p], in_sem.at[0, p]),
            pltpu.make_async_copy(kappa_ref.at[p], dinv.at[p], in_sem.at[1, p]),
        ]
        for copy in loads[p]:
            copy.start()

    barrier = pltpu.get_barrier_semaphore()

    @pl.loop(1, n)
    def _(step):
        pl.semaphore_signal(
            barrier, inc=1, device_id={"gx": lax.rem(me + step, n)}, device_id_type=MESH
        )

    lane = lax.broadcasted_iota(jnp.int32, (ROWS, LANES), 1)
    first, last = lane == 0, lane == LANES - 1
    z = lax.broadcasted_iota(jnp.int32, (ROWS, nz), 1)
    for level in range(SWEEPS):
        for p in range(slab):
            u[level, p + 1, pl.ds(0, PAD), :] = jnp.zeros((PAD, nz), jnp.float32)
            u[level, p + 1, pl.ds(PAD + ny, PAD), :] = jnp.zeros((PAD, nz), jnp.float32)

    for edge, place in ((0, 0), (n - 1, slab + 1)):

        @pl.when(me == edge)
        def _():
            for level in range(SWEEPS):

                @pl.loop(0, ny // ROWS)
                def _(tile):
                    y = pl.multiple_of(tile * ROWS, ROWS)
                    u[level, place, pl.ds(y + PAD, ROWS), :] = jnp.zeros((ROWS, nz), jnp.float32)

    height = ny // CHUNKS

    def transfer(level, side, chunk):
        rows = pl.ds(PAD + chunk * height, height)
        return pltpu.make_async_remote_copy(
            src_ref=u.at[level, slab if side else 1, rows],
            dst_ref=u.at[level, 0 if side else slab + 1, rows],
            send_sem=send_sem.at[level, side, chunk],
            recv_sem=recv_sem.at[level, side, chunk],
            device_id={"gx": lax.rem(me + (1 if side else n - 1), n)},
            device_id_type=MESH,
        )

    def sends(side):
        return me < n - 1 if side else me > 0

    def receives(side):
        return me > 0 if side else me < n - 1

    def send(level, chunk):
        for side in range(2):

            @pl.when(sends(side))
            def _():
                transfer(level, side, chunk).start()

    def await_halo(level, chunk):
        for side in range(2):

            @pl.when(receives(side))
            def _():
                transfer(level, side, chunk).wait_recv()

    def prepare(p, y, rows):
        inside = z < depth_ref[rows, p : p + 1]
        inv = jnp.where(inside, 1.0 / (dinv[p, rows, :] + 12.0), 0.0)
        masked = jnp.where(inside, data[p, rows, :], 0.0)
        dinv[p, rows, :] = inv
        u[0, p + 1, pl.ds(y + PAD, ROWS), :] = inv * masked
        return masked

    blocks_y = ny // BY
    sums = [jnp.zeros((PAD, nz), jnp.float32) for _ in range(blocks_y)]

    def fold(planes, sums):
        for p in planes:
            for copy in loads[p]:
                copy.wait()
        for j in range(blocks_y):

            def body(tile, total):
                y = pl.multiple_of(j * BY + tile * ROWS, ROWS)
                rows = pl.ds(y, ROWS)
                for p in planes:
                    masked = prepare(p, y, rows)
                    for r in range(0, ROWS, PAD):
                        total = total + masked[r : r + PAD]
                return total

            sums[j] = lax.fori_loop(0, BY // ROWS, body, sums[j])
        return sums

    sums = fold([0, slab - 1], sums)
    pl.semaphore_wait(barrier, n - 1)
    for chunk in range(CHUNKS):
        send(0, chunk)
    for pair in range(2, slab, 2):
        sums = fold(order[pair : pair + 2], sums)

    blocks_z = nz // BZ
    blocks = blocks_y * blocks_z
    count = inverse_ref.shape[0]
    onehot = (
        agg_ref[...] == lax.broadcasted_iota(jnp.int32, (blocks, count), 1)
    ).astype(jnp.float32)
    spread = (
        lax.broadcasted_iota(jnp.int32, (blocks_z, nz), 1) // BZ
        == lax.broadcasted_iota(jnp.int32, (blocks_z, nz), 0)
    ).astype(jnp.float32)
    rhs = jnp.zeros((1, count), jnp.float32)
    for j in range(blocks_y):
        row = jnp.sum(sums[j], axis=0, keepdims=True) / BLOCK_CELLS
        per_block = jnp.sum(spread * row, axis=1, keepdims=True)
        rhs = rhs + jnp.sum(onehot[j * blocks_z : (j + 1) * blocks_z] * per_block, axis=0, keepdims=True)
    part[...] = jnp.broadcast_to(rhs, part.shape)

    def part_copy(step):
        return pltpu.make_async_remote_copy(
            src_ref=part,
            dst_ref=parts.at[step],
            send_sem=part_send.at[step],
            recv_sem=part_recv.at[step],
            device_id={"gx": lax.rem(me + step, n)},
            device_id_type=MESH,
        )

    @pl.loop(1, n)
    def _(step):
        part_copy(step).start()

    def advance(level, planes, y):
        for p in planes:
            rows = pl.ds(y + PAD, ROWS)
            around = in_plane(u, (level, p + 1), y, first, last)
            across = u[level, p, rows, :] + u[level, p + 2, rows, :]
            yield p, u[0, p + 1, rows, :] + dinv[p, pl.ds(y, ROWS), :] * (around + 4.0 * across)

    def sweep(level, planes, begin, end):
        @pl.loop(begin // ROWS, end // ROWS)
        def _(tile):
            y = pl.multiple_of(tile * ROWS, ROWS)
            for p, value in advance(level, planes, y):
                u[level + 1, p + 1, pl.ds(y + PAD, ROWS), :] = value

    edges, inner = [0, slab - 1], list(range(1, slab - 1))
    for level in range(SWEEPS - 1):
        sweep(level, inner, 0, ny)
        for chunk in range(CHUNKS):
            await_halo(level, chunk)
            sweep(level, edges, chunk * height, (chunk + 1) * height)
            send(level + 1, chunk)

    @pl.loop(1, n)
    def _(step):
        part_copy(step).wait_recv()

    rhs = lax.fori_loop(1, n, lambda step, total: total + parts[step], part[...])
    solved = lax.dot_general(
        rhs, inverse_ref[...], (((1,), (1,)), ((), ())),
        precision=HIGHEST, preferred_element_type=jnp.float32,
    )[:1]
    coarse = jnp.sum(onehot * solved, axis=1, keepdims=True)
    coarse_rows = [
        jnp.sum(spread * coarse[j * blocks_z : (j + 1) * blocks_z], axis=0, keepdims=True)
        for j in range(blocks_y)
    ]

    def finish(planes, begin, end):
        for j in range(blocks_y):
            low, high = max(begin, j * BY), min(end, (j + 1) * BY)
            if low >= high:
                continue

            @pl.loop(low // ROWS, high // ROWS)
            def _(tile):
                y = pl.multiple_of(tile * ROWS, ROWS)
                rows = pl.ds(y, ROWS)
                for p, value in advance(SWEEPS - 1, planes, y):
                    inside = z < depth_ref[rows, p : p + 1]
                    data[p, rows, :] = value + jnp.where(inside, coarse_rows[j], 0.0)

    finish(inner, 0, ny)
    inner_out = pltpu.make_async_copy(
        data.at[pl.ds(1, slab - 2)], out_ref.at[pl.ds(1, slab - 2)], out_sem.at[0]
    )
    inner_out.start()
    outs = [inner_out]
    for chunk in range(CHUNKS):
        await_halo(SWEEPS - 1, chunk)
        finish(edges, chunk * height, (chunk + 1) * height)
        for p in edges:
            rows = pl.ds(chunk * height, height)
            copy = pltpu.make_async_copy(
                data.at[p, rows], out_ref.at[p, rows], out_sem.at[len(outs)]
            )
            copy.start()
            outs.append(copy)
    for copy in outs:
        copy.wait()
    for level in range(SWEEPS):
        for chunk in range(CHUNKS):
            for side in range(2):

                @pl.when(sends(side))
                def _():
                    transfer(level, side, chunk).wait_send()

    @pl.loop(1, n)
    def _(step):
        part_copy(step).wait_send()


def on_device(right_side, kappa_sq, depth, agg_ids, coarse_inverse):
    n = lax.axis_size("gx")
    slab, ny, nz = right_side.shape
    count = coarse_inverse.shape[0]
    vmem, anywhere = pl.BlockSpec(memory_space=pltpu.VMEM), pl.BlockSpec(memory_space=pl.ANY)
    return pl.pallas_call(
        functools.partial(kernel, n),
        out_shape=jax.ShapeDtypeStruct(right_side.shape, jnp.float32),
        in_specs=[anywhere, anywhere, vmem, vmem, vmem],
        out_specs=anywhere,
        scratch_shapes=[
            pltpu.VMEM((SWEEPS, slab + 2, ny + 2 * PAD, nz), jnp.float32),
            pltpu.VMEM((slab, ny, nz), jnp.float32),
            pltpu.VMEM((slab, ny, nz), jnp.float32),
            pltpu.VMEM((8, count), jnp.float32),
            pltpu.VMEM((n, 8, count), jnp.float32),
            pltpu.SemaphoreType.DMA((2, slab)),
            pltpu.SemaphoreType.DMA((SWEEPS, 2, CHUNKS)),
            pltpu.SemaphoreType.DMA((SWEEPS, 2, CHUNKS)),
            pltpu.SemaphoreType.DMA((n,)),
            pltpu.SemaphoreType.DMA((n,)),
            pltpu.SemaphoreType.DMA((1 + 2 * CHUNKS,)),
        ],
        compiler_params=pltpu.CompilerParams(
            collective_id=0, has_side_effects=True, vmem_limit_bytes=56 * 1024 * 1024
        ),
    )(right_side, kappa_sq, depth.T, agg_ids[:, None], coarse_inverse)


def solution(mesh):
    in_specs = (
        P(("groups", "gx"), None, None),
        P(("groups", "gx"), None, None),
        P(("groups", "gx"), None),
        P(("groups", "gx")),
        P("groups", None),
    )
    out_specs = P(("groups", "gx"), None, None)
    return jax.shard_map(
        on_device, mesh=mesh, in_specs=in_specs, out_specs=out_specs, check_vma=False
    )
```

time: 247 us -> 66.2 us (0.27); the launches traced: 242 us -> 66 us
  other arithmetic: 119 us -> 0 us
  blocking collectives: 59.7 us -> 0 us
  Pallas kernels: 0 us -> 58.5 us
  waiting for transfers between devices: 45.1 us -> 0 us
  starting transfers between devices: 10.4 us -> 0 us
    mul x5 -> x0, other arithmetic: 110 us -> none  [the longest x4 83.1 us: on_device(): field = source + local_mask * neighbour_sum(ext * field)]
    psum x1 -> x0, blocking collectives: 59.7 us -> none  [on_device(): coarse_rhs = lax.psum(partial_rhs, 'gx')]
    pallas_call x0 -> x1, Pallas kernels: none -> 58.5 us  [on_device(): pl.pallas_call(functools.partial(kernel, n), out_shape=jax.ShapeDtypeStru...]
    ppermute x4 -> x0, waiting for transfers between devices: 45.1 us -> none  [the longest x1 43.5 us: extended(): lax.ppermute(tail, axis, [(i, (i + 1) % count) for i in range(ends)])]
    ppermute x4 -> x0, starting transfers between devices: 10.4 us -> none  [the longest x2 4.74 us: from_behind(): lax.ppermute(value, axis, [(source, source + steps) for source in range(f...]
    slice x2 -> x0, local copies, waits for them, and re-layouts: 5.15 us -> none  [the longest x1 4.7 us: on_device(): upper_rim = solved[MARGIN + slab:]]
    add x1 -> x0, other arithmetic: 5.11 us -> none  [on_device(): return fine + mask * coarse]
    unnamed x12 -> x2, local copies, waits for them, and re-layouts: 1.36 us -> 6.13 us
  transfers between devices with their start and end apart: 4 -> 0, of which waited for: 2 -> 0; matrix products, arithmetic and copies ran while one was open for 1% -> 0% of each run, Pallas kernels for 0% -> 0%
where the time goes in v1:
time: 66.2 us; the launch traced here: 66 us
  Pallas kernels  58.5 us (88%)
  local copies, waits for them, and re-layouts  7.45 us (11%)
    pallas_call x1, Pallas kernels, on_device(): pl.pallas_call(functools.partial(kernel, n), out_shape=jax.ShapeDtypeStru...  58.5 us
    unnamed x2, local copies, waits for them, and re-layouts  6.13 us
    broadcast_in_dim x1, local copies, waits for them, and re-layouts, on_device(): agg_ids[:, None]  1.33 us

profile of v1, /device:TPU:9, one launch (start us, length us, event | category | flops | bytes accessed | tf_op | source)
XLA Modules:
  0.0 66.0 jit_solution(17391865972110722888)
XLA Ops:
  0.0 1.3 %copy.7.agg_ref = s32[32,1]{1,0:T(8,128)} copy(s32[32,1]{0,1:T(1,128)} %bitcast.3) | data formatting | bytes 256 | tf_op jit(solution)/shard_map/broadcast_in_dim | solution.py:294
  1.3 1.5 %copy.6 = s32[8,256]{0,1:T(8,128)} copy(s32[8,256]{1,0:T(8,128)} %param.7) | data formatting | bytes 16384 | tf_op args[2]
  2.8 58.5 %shard_map.55 = f32[8,256,512]{2,1,0:T(8,128)} custom-call(f32[8,256,512]{2,1,0:T(8,128)} %right_ref.1, f32[8,256,512]{2,1,0:T(8,128)} %kappa_ref.1, s32[256,8]{1,0:T(8,128)} %bitcast.2, s32[32,1]{1,0:T(8,128)} %copy.7.agg_ref, f32[256,256]{1,0:T(8,128)} %inverse_ref.1), custom_call_target="tpu_custom_call" | custom-call | tf_op jit(solution)/shard_map/pallas_call | solution.py:273
  61.4 4.6 %copy.9 = f32[8,256,512]{2,1,0:T(8,128)} copy(f32[8,256,512]{2,1,0:T(8,128)} %shard_map.55) | data formatting | bytes 8388608

commit v2 on v1

v2 whole, which is shorter than its diff:
```python
import functools

import jax
import jax.numpy as jnp
from jax import lax
from jax.experimental import pallas as pl
from jax.experimental.pallas import tpu as pltpu
from jax.sharding import PartitionSpec as P

SWEEPS = 4
BY = 64
BZ = 64
BLOCK_CELLS = 32768
SUB = 8
LANES = 128
CHUNKS = 2
MESH = pl.DeviceIdType.MESH
HIGHEST = lax.Precision.HIGHEST


def kernel(
    n, right_ref, kappa_ref, depth_ref, agg_ref, inverse_ref, out_ref,
    u, dinv, data, kappa, part, parts, in_sem, send_sem, recv_sem, part_send, part_recv, out_sem,
):
    slab, ny, nz = right_ref.shape
    steps, cols = ny // SUB, nz // LANES
    me = lax.axis_index("gx")
    order = [p for pair in zip(range(slab // 2), range(slab - 1, slab // 2 - 1, -1)) for p in pair]

    def column(i):
        return pl.ds(i * LANES, LANES)

    loads = {}
    for p in order:
        loads[p] = []
        for i in range(cols):
            source = (p, slice(None), column(i))
            loads[p].append(
                pltpu.make_async_copy(kappa_ref.at[source], kappa.at[p, i], in_sem.at[0, p, i])
            )
            loads[p].append(
                pltpu.make_async_copy(right_ref.at[source], data.at[p, i], in_sem.at[1, p, i])
            )
        for copy in loads[p]:
            copy.start()

    barrier = pltpu.get_barrier_semaphore()

    @pl.loop(1, n)
    def _(step):
        pl.semaphore_signal(
            barrier, inc=1, device_id={"gx": lax.rem(me + step, n)}, device_id_type=MESH
        )

    tile = (SUB, LANES)
    lane = lax.broadcasted_iota(jnp.int32, tile, 1)
    sub = lax.broadcasted_iota(jnp.int32, tile, 0)
    first, last = lane == 0, lane == LANES - 1
    top, bottom = sub == 0, sub == SUB - 1
    zero = jnp.zeros(tile, jnp.float32)

    for edge, place in ((0, 0), (n - 1, slab + 1)):

        @pl.when(me == edge)
        def _():
            @pl.loop(0, steps)
            def _(j):
                for level in range(SWEEPS):
                    for i in range(cols):
                        u[level, place, i, j + 1] = zero

    height = steps // CHUNKS

    def transfer(level, side, chunk):
        rows = pl.ds(1 + chunk * height, height)
        return pltpu.make_async_remote_copy(
            src_ref=u.at[level, slab if side else 1, :, rows],
            dst_ref=u.at[level, 0 if side else slab + 1, :, rows],
            send_sem=send_sem.at[level, side, chunk],
            recv_sem=recv_sem.at[level, side, chunk],
            device_id={"gx": lax.rem(me + (1 if side else n - 1), n)},
            device_id_type=MESH,
        )

    def sends(side):
        return me < n - 1 if side else me > 0

    def receives(side):
        return me > 0 if side else me < n - 1

    def send(level, chunk):
        for side in range(2):

            @pl.when(sends(side))
            def _():
                transfer(level, side, chunk).start()

    def await_halo(level, chunk):
        for side in range(2):

            @pl.when(receives(side))
            def _():
                transfer(level, side, chunk).wait_recv()

    def wrap(level, planes):
        for p in planes:
            for i in range(cols):
                before = pltpu.roll(u[level, p + 1, i, steps], 1, 0)
                after = pltpu.roll(u[level, p + 1, i, 1], SUB - 1, 0)
                u[level, p + 1, i, 0] = jnp.where(top, 0.0, before)
                u[level, p + 1, i, steps + 1] = jnp.where(bottom, 0.0, after)

    place = lax.broadcasted_iota(jnp.int32, (SUB, ny), 1) - steps * lax.broadcasted_iota(
        jnp.int32, (SUB, ny), 0
    )
    zs = [(lane + i * LANES).astype(jnp.float32) for i in range(cols)]

    def fold(planes, totals):
        for p in planes:
            for copy in loads[p]:
                copy.wait()
        depths = [
            jnp.broadcast_to(depth_ref[p : p + 1, :].astype(jnp.float32), (SUB, ny))
            for p in planes
        ]

        def body(j, totals):
            totals = list(totals)
            rows = pl.ds(j, SUB, stride=steps)
            for p, line in zip(planes, depths):
                depth = jnp.sum(jnp.where(place == j, line, 0.0), axis=1, keepdims=True)
                for i in range(cols):
                    inside = zs[i] < depth
                    inv = jnp.where(inside, 1.0 / (kappa[p, i, rows, :] + 12.0), 0.0)
                    masked = jnp.where(inside, data[p, i, rows, :], 0.0)
                    dinv[p, i, j] = inv
                    u[0, p + 1, i, j + 1] = inv * masked
                    totals[i] = totals[i] + masked
            return tuple(totals)

        return lax.fori_loop(0, steps, body, totals)

    edges, inner = [0, slab - 1], list(range(1, slab - 1))
    totals = fold(edges, (zero,) * cols)
    pl.semaphore_wait(barrier, n - 1)
    for chunk in range(CHUNKS):
        send(0, chunk)
    for pair in range(2, slab, 2):
        totals = fold(order[pair : pair + 2], totals)
    wrap(0, range(slab))

    blocks_y, blocks_z = ny // BY, nz // BZ
    blocks = blocks_y * blocks_z
    parts_per_block, blocks_per_col = BY // steps, LANES // BZ
    count = inverse_ref.shape[0]
    square = (blocks, blocks)
    diagonal = lax.broadcasted_iota(jnp.int32, square, 0) == lax.broadcasted_iota(
        jnp.int32, square, 1
    )
    ids = jnp.sum(
        jnp.where(diagonal, agg_ref[...].astype(jnp.float32), 0.0), axis=1, keepdims=True
    )
    onehot = (
        ids == lax.broadcasted_iota(jnp.int32, (blocks, count), 1).astype(jnp.float32)
    ).astype(jnp.float32)

    def members(j, k):
        return (sub // parts_per_block == j) & (lane // BZ == k % blocks_per_col)

    rhs = jnp.zeros((1, count), jnp.float32)
    for j in range(blocks_y):
        for k in range(blocks_z):
            picked = jnp.where(members(j, k), totals[k // blocks_per_col], 0.0)
            block = jnp.sum(jnp.sum(picked, axis=1, keepdims=True), axis=0, keepdims=True)
            b = j * blocks_z + k
            rhs = rhs + onehot[b : b + 1] * (block / BLOCK_CELLS)
    part[...] = jnp.broadcast_to(rhs, part.shape)

    def part_copy(step):
        return pltpu.make_async_remote_copy(
            src_ref=part,
            dst_ref=parts.at[step],
            send_sem=part_send.at[step],
            recv_sem=part_recv.at[step],
            device_id={"gx": lax.rem(me + step, n)},
            device_id_type=MESH,
        )

    @pl.loop(1, n)
    def _(step):
        part_copy(step).start()

    def advance(level, planes, j):
        held = {}

        def tiles(p):
            if p not in held:
                held[p] = [u[level, p, i, j + 1] for i in range(cols)]
            return held[p]

        for p in planes:
            before, mid, after = tiles(p), tiles(p + 1), tiles(p + 2)
            right = [pltpu.roll(c, 1, 1) for c in mid]
            left = [pltpu.roll(c, LANES - 1, 1) for c in mid]
            values = []
            for i in range(cols):
                below = jnp.where(first, right[i - 1] if i else zero, right[i])
                above = jnp.where(last, left[i + 1] if i + 1 < cols else zero, left[i])
                around = (u[level, p + 1, i, j] + u[level, p + 1, i, j + 2]) + (below + above)
                total = around + 4.0 * (before[i] + after[i])
                values.append(u[0, p + 1, i, j + 1] + dinv[p, i, j] * total)
            yield p, values

    def sweep(level, planes, begin, end):
        @pl.loop(begin, end)
        def _(j):
            for p, values in advance(level, planes, j):
                for i in range(cols):
                    u[level + 1, p + 1, i, j + 1] = values[i]

    for level in range(SWEEPS - 1):
        sweep(level, inner, 0, steps)
        wrap(level + 1, inner)
        for chunk in range(CHUNKS):
            await_halo(level, chunk)
            sweep(level, edges, chunk * height, (chunk + 1) * height)
            send(level + 1, chunk)
        wrap(level + 1, edges)

    @pl.loop(1, n)
    def _(step):
        part_copy(step).wait_recv()

    rhs = lax.fori_loop(1, n, lambda step, total: total + parts[step], part[...])
    solved = lax.dot_general(
        rhs, inverse_ref[...], (((1,), (1,)), ((), ())),
        precision=HIGHEST, preferred_element_type=jnp.float32,
    )[:1]
    coarse = jnp.sum(onehot * solved, axis=1, keepdims=True)
    added = [zero] * cols
    for j in range(blocks_y):
        for k in range(blocks_z):
            b, i = j * blocks_z + k, k // blocks_per_col
            added[i] = jnp.where(members(j, k), coarse[b : b + 1], added[i])

    def finish(planes, begin, end):
        @pl.loop(begin, end)
        def _(j):
            for p, values in advance(SWEEPS - 1, planes, j):
                for i in range(cols):
                    data[p, i, pl.ds(j, SUB, stride=steps), :] = values[i] + jnp.where(
                        dinv[p, i, j] > 0, added[i], 0.0
                    )

    def write(planes):
        copies = []
        for p in planes:
            for i in range(cols):
                copies.append(
                    pltpu.make_async_copy(
                        data.at[p, i], out_ref.at[p, :, column(i)], out_sem.at[p, i]
                    )
                )
                copies[-1].start()
        return copies

    finish(inner, 0, steps)
    outs = write(inner)
    for chunk in range(CHUNKS):
        await_halo(SWEEPS - 1, chunk)
        finish(edges, chunk * height, (chunk + 1) * height)
    outs += write(edges)
    for copy in outs:
        copy.wait()
    for level in range(SWEEPS):
        for chunk in range(CHUNKS):
            for side in range(2):

                @pl.when(sends(side))
                def _():
                    transfer(level, side, chunk).wait_send()

    @pl.loop(1, n)
    def _(step):
        part_copy(step).wait_send()


def on_device(right_side, kappa_sq, depth, agg_ids, coarse_inverse):
    n = lax.axis_size("gx")
    slab, ny, nz = right_side.shape
    steps, cols = ny // SUB, nz // LANES
    count = coarse_inverse.shape[0]
    vmem, anywhere = pl.BlockSpec(memory_space=pltpu.VMEM), pl.BlockSpec(memory_space=pl.ANY)
    return pl.pallas_call(
        functools.partial(kernel, n),
        out_shape=jax.ShapeDtypeStruct(right_side.shape, jnp.float32),
        in_specs=[anywhere, anywhere, vmem, vmem, vmem],
        out_specs=anywhere,
        scratch_shapes=[
            pltpu.VMEM((SWEEPS, slab + 2, cols, steps + 2, SUB, LANES), jnp.float32),
            pltpu.VMEM((slab, cols, steps, SUB, LANES), jnp.float32),
            pltpu.VMEM((slab, cols, ny, LANES), jnp.float32),
            pltpu.VMEM((slab, cols, ny, LANES), jnp.float32),
            pltpu.VMEM((8, count), jnp.float32),
            pltpu.VMEM((n, 8, count), jnp.float32),
            pltpu.SemaphoreType.DMA((2, slab, cols)),
            pltpu.SemaphoreType.DMA((SWEEPS, 2, CHUNKS)),
            pltpu.SemaphoreType.DMA((SWEEPS, 2, CHUNKS)),
            pltpu.SemaphoreType.DMA((n,)),
            pltpu.SemaphoreType.DMA((n,)),
            pltpu.SemaphoreType.DMA((slab, cols)),
        ],
        compiler_params=pltpu.CompilerParams(
            collective_id=0, has_side_effects=True, vmem_limit_bytes=56 * 1024 * 1024
        ),
    )(right_side, kappa_sq, depth, agg_ids[None, :], coarse_inverse)


def solution(mesh):
    in_specs = (
        P(("groups", "gx"), None, None),
        P(("groups", "gx"), None, None),
        P(("groups", "gx"), None),
        P(("groups", "gx")),
        P("groups", None),
    )
    out_specs = P(("groups", "gx"), None, None)
    return jax.shard_map(
        on_device, mesh=mesh, in_specs=in_specs, out_specs=out_specs, check_vma=False
    )
```

time: 66.2 us -> 69.4 us (1.048)
  Pallas kernels: 58.5 us -> 64.6 us
  local copies, waits for them, and re-layouts: 7.45 us -> 4.64 us
    pallas_call x1, Pallas kernels: 58.5 us -> 64.6 us  [on_device(): pl.pallas_call(functools.partial(kernel, n), out_shape=jax.ShapeDtypeStru...]
    unnamed x2 -> x1, local copies, waits for them, and re-layouts: 6.13 us -> 4.64 us
    broadcast_in_dim x1 -> x0, local copies, waits for them, and re-layouts: 1.33 us -> none  [on_device(): agg_ids[:, None]]
where the time goes in v2:
time: 69.4 us; the launch traced here: 69.2 us
  Pallas kernels  64.6 us (93%)
  local copies, waits for them, and re-layouts  4.64 us (7%)
    pallas_call x1, Pallas kernels, on_device(): pl.pallas_call(functools.partial(kernel, n), out_shape=jax.ShapeDtypeStru...  64.6 us
    unnamed x1, local copies, waits for them, and re-layouts  4.64 us

profile of v2, /device:TPU:9, one launch (start us, length us, event | category | flops | bytes accessed | tf_op | source)
XLA Modules:
  0.0 69.2 jit_solution(564636991244506121)
XLA Ops:
  0.0 64.6 %shard_map.55 = f32[8,256,512]{2,1,0:T(8,128)} custom-call(f32[8,256,512]{2,1,0:T(8,128)} %right_ref.1, f32[8,256,512]{2,1,0:T(8,128)} %kappa_ref.1, s32[8,256]{1,0:T(8,128)} %depth_ref.1, s32[1,32]{1,0:T(1,128)} %bitcast.1, f32[256,256]{1,0:T(8,128)} %inverse_ref.1), custom_call_target="tpu_custom_call" | custom-call | tf_op jit(solution)/shard_map/pallas_call | solution.py:294
  64.6 4.6 %copy.7 = f32[8,256,512]{2,1,0:T(8,128)} copy(f32[8,256,512]{2,1,0:T(8,128)} %shard_map.55) | data formatting | bytes 8388608

commit v3 on v2

--- a/solution.py
+++ b/solution.py
@@ -13,17 +13,18 @@
 BLOCK_CELLS = 32768
 SUB = 8
 LANES = 128
-CHUNKS = 2
+CHUNKS = 4
 MESH = pl.DeviceIdType.MESH
 HIGHEST = lax.Precision.HIGHEST
 
 
 def kernel(
     n, right_ref, kappa_ref, depth_ref, agg_ref, inverse_ref, out_ref,
-    u, dinv, data, kappa, part, parts, in_sem, send_sem, recv_sem, part_send, part_recv, out_sem,
+    u0, u1, u2, u3, dinv, data, kappa, part, parts, in_sem, send_sem, recv_sem, part_send, part_recv, out_sem,
 ):
     slab, ny, nz = right_ref.shape
     steps, cols = ny // SUB, nz // LANES
+    u = (u0, u1, u2, u3)
     me = lax.axis_index("gx")
     order = [p for pair in zip(range(slab // 2), range(slab - 1, slab // 2 - 1, -1)) for p in pair]
 
@@ -67,15 +68,15 @@
             def _(j):
                 for level in range(SWEEPS):
                     for i in range(cols):
-                        u[level, place, i, j + 1] = zero
+                        u[level][place, i, j + 1] = zero
 
     height = steps // CHUNKS
 
     def transfer(level, side, chunk):
         rows = pl.ds(1 + chunk * height, height)
         return pltpu.make_async_remote_copy(
-            src_ref=u.at[level, slab if side else 1, :, rows],
-            dst_ref=u.at[level, 0 if side else slab + 1, :, rows],
+            src_ref=u[level].at[slab if side else 1, :, rows],
+            dst_ref=u[level].at[0 if side else slab + 1, :, rows],
             send_sem=send_sem.at[level, side, chunk],
             recv_sem=recv_sem.at[level, side, chunk],
             device_id={"gx": lax.rem(me + (1 if side else n - 1), n)},
@@ -105,48 +106,71 @@
     def wrap(level, planes):
         for p in planes:
             for i in range(cols):
-                before = pltpu.roll(u[level, p + 1, i, steps], 1, 0)
-                after = pltpu.roll(u[level, p + 1, i, 1], SUB - 1, 0)
-                u[level, p + 1, i, 0] = jnp.where(top, 0.0, before)
-                u[level, p + 1, i, steps + 1] = jnp.where(bottom, 0.0, after)
+                before = pltpu.roll(u[level][p + 1, i, steps], 1, 0)
+                after = pltpu.roll(u[level][p + 1, i, 1], SUB - 1, 0)
+                u[level][p + 1, i, 0] = jnp.where(top, 0.0, before)
+                u[level][p + 1, i, steps + 1] = jnp.where(bottom, 0.0, after)
 
     place = lax.broadcasted_iota(jnp.int32, (SUB, ny), 1) - steps * lax.broadcasted_iota(
         jnp.int32, (SUB, ny), 0
     )
     zs = [(lane + i * LANES).astype(jnp.float32) for i in range(cols)]
 
-    def fold(planes, totals):
+    def swap(tiles):
+        for d in (4, 2, 1):
+            low = (sub // d) % 2 == 0
+            tiles = list(tiles)
+            for k in range(SUB):
+                if k // d % 2 == 0:
+                    x, y = tiles[k], tiles[k + d]
+                    tiles[k] = jnp.where(low, x, pltpu.roll(y, d, 0))
+                    tiles[k + d] = jnp.where(low, pltpu.roll(x, SUB - d, 0), y)
+        return tiles
+
+    def arrive(planes):
         for p in planes:
             for copy in loads[p]:
                 copy.wait()
-        depths = [
+
+    def fold(planes, totals, begin, end):
+        lines = [
             jnp.broadcast_to(depth_ref[p : p + 1, :].astype(jnp.float32), (SUB, ny))
             for p in planes
         ]
 
-        def body(j, totals):
+        def body(group, totals):
             totals = list(totals)
-            rows = pl.ds(j, SUB, stride=steps)
-            for p, line in zip(planes, depths):
-                depth = jnp.sum(jnp.where(place == j, line, 0.0), axis=1, keepdims=True)
+            j = group * SUB
+            rows = [pl.ds(pl.multiple_of(s * steps + j, SUB), SUB) for s in range(SUB)]
+            for p, line in zip(planes, lines):
+                depths = [
+                    jnp.sum(jnp.where(place == j + k, line, 0.0), axis=1, keepdims=True)
+                    for k in range(SUB)
+                ]
                 for i in range(cols):
-                    inside = zs[i] < depth
-                    inv = jnp.where(inside, 1.0 / (kappa[p, i, rows, :] + 12.0), 0.0)
-                    masked = jnp.where(inside, data[p, i, rows, :], 0.0)
-                    dinv[p, i, j] = inv
-                    u[0, p + 1, i, j + 1] = inv * masked
-                    totals[i] = totals[i] + masked
+                    scales = swap([kappa[p, i, r, :] for r in rows])
+                    values = swap([data[p, i, r, :] for r in rows])
+                    for k in range(SUB):
+                        inside = zs[i] < depths[k]
+                        inv = jnp.where(inside, 1.0 / (scales[k] + 12.0), 0.0)
+                        masked = jnp.where(inside, values[k], 0.0)
+                        dinv[p, i, j + k] = inv
+                        u0[p + 1, i, j + k + 1] = inv * masked
+                        totals[i] = totals[i] + masked
             return tuple(totals)
 
-        return lax.fori_loop(0, steps, body, totals)
+        return lax.fori_loop(begin // SUB, end // SUB, body, totals)
 
     edges, inner = [0, slab - 1], list(range(1, slab - 1))
-    totals = fold(edges, (zero,) * cols)
+    totals = (zero,) * cols
     pl.semaphore_wait(barrier, n - 1)
+    arrive(edges)
     for chunk in range(CHUNKS):
+        totals = fold(edges, totals, chunk * height, (chunk + 1) * height)
         send(0, chunk)
     for pair in range(2, slab, 2):
-        totals = fold(order[pair : pair + 2], totals)
+        arrive(order[pair : pair + 2])
+        totals = fold(order[pair : pair + 2], totals, 0, steps)
     wrap(0, range(slab))
 
     blocks_y, blocks_z = ny // BY, nz // BZ
@@ -195,7 +219,7 @@
 
         def tiles(p):
             if p not in held:
-                held[p] = [u[level, p, i, j + 1] for i in range(cols)]
+                held[p] = [u[level][p, i, j + 1] for i in range(cols)]
             return held[p]
 
         for p in planes:
@@ -206,9 +230,9 @@
             for i in range(cols):
                 below = jnp.where(first, right[i - 1] if i else zero, right[i])
                 above = jnp.where(last, left[i + 1] if i + 1 < cols else zero, left[i])
-                around = (u[level, p + 1, i, j] + u[level, p + 1, i, j + 2]) + (below + above)
+                around = (u[level][p + 1, i, j] + u[level][p + 1, i, j + 2]) + (below + above)
                 total = around + 4.0 * (before[i] + after[i])
-                values.append(u[0, p + 1, i, j + 1] + dinv[p, i, j] * total)
+                values.append(u0[p + 1, i, j + 1] + dinv[p, i, j] * total)
             yield p, values
 
     def sweep(level, planes, begin, end):
@@ -216,16 +240,15 @@
         def _(j):
             for p, values in advance(level, planes, j):
                 for i in range(cols):
-                    u[level + 1, p + 1, i, j + 1] = values[i]
+                    u[level + 1][p + 1, i, j + 1] = values[i]
 
     for level in range(SWEEPS - 1):
-        sweep(level, inner, 0, steps)
-        wrap(level + 1, inner)
         for chunk in range(CHUNKS):
             await_halo(level, chunk)
             sweep(level, edges, chunk * height, (chunk + 1) * height)
             send(level + 1, chunk)
-        wrap(level + 1, edges)
+            sweep(level, inner, chunk * height, (chunk + 1) * height)
+        wrap(level + 1, range(slab))
 
     @pl.loop(1, n)
     def _(step):
@@ -244,13 +267,22 @@
             added[i] = jnp.where(members(j, k), coarse[b : b + 1], added[i])
 
     def finish(planes, begin, end):
-        @pl.loop(begin, end)
-        def _(j):
-            for p, values in advance(SWEEPS - 1, planes, j):
+        for p in planes:
+
+            @pl.loop(begin // SUB, end // SUB)
+            def _(group):
+                j = group * SUB
+                results = [[] for _ in range(cols)]
+                for k in range(SUB):
+                    for _, values in advance(SWEEPS - 1, [p], j + k):
+                        for i in range(cols):
+                            results[i].append(
+                                values[i] + jnp.where(dinv[p, i, j + k] > 0, added[i], 0.0)
+                            )
                 for i in range(cols):
-                    data[p, i, pl.ds(j, SUB, stride=steps), :] = values[i] + jnp.where(
-                        dinv[p, i, j] > 0, added[i], 0.0
-                    )
+                    for s, value in enumerate(swap(results[i])):
+                        rows = pl.ds(pl.multiple_of(s * steps + j, SUB), SUB)
+                        data[p, i, rows, :] = value
 
     def write(planes):
         copies = []
@@ -297,7 +329,7 @@
         in_specs=[anywhere, anywhere, vmem, vmem, vmem],
         out_specs=anywhere,
         scratch_shapes=[
-            pltpu.VMEM((SWEEPS, slab + 2, cols, steps + 2, SUB, LANES), jnp.float32),
+            *[pltpu.VMEM((slab + 2, cols, steps + 2, SUB, LANES), jnp.float32)] * SWEEPS,
             pltpu.VMEM((slab, cols, steps, SUB, LANES), jnp.float32),
             pltpu.VMEM((slab, cols, ny, LANES), jnp.float32),
             pltpu.VMEM((slab, cols, ny, LANES), jnp.float32),

time: 69.4 us -> 64 us (0.922)
  Pallas kernels: 64.6 us -> 58.7 us
    pallas_call x1, Pallas kernels: 64.6 us -> 58.7 us  [on_device(): pl.pallas_call(functools.partial(kernel, n), out_shape=jax.ShapeDtypeStru...]
where the time goes in v3:
time: 64 us; the launch traced here: 63.3 us
  Pallas kernels  58.7 us (92%)
  local copies, waits for them, and re-layouts  4.64 us (7%)
    pallas_call x1, Pallas kernels, on_device(): pl.pallas_call(functools.partial(kernel, n), out_shape=jax.ShapeDtypeStru...  58.7 us
    unnamed x1, local copies, waits for them, and re-layouts  4.64 us

profile of v3, /device:TPU:9, one launch (start us, length us, event | category | flops | bytes accessed | tf_op | source)
XLA Modules:
  0.0 63.3 jit_solution(5077712000012544206)
XLA Ops:
  0.0 58.7 %shard_map.55 = f32[8,256,512]{2,1,0:T(8,128)} custom-call(f32[8,256,512]{2,1,0:T(8,128)} %right_ref.1, f32[8,256,512]{2,1,0:T(8,128)} %kappa_ref.1, s32[8,256]{1,0:T(8,128)} %depth_ref.1, s32[1,32]{1,0:T(1,128)} %bitcast.1, f32[256,256]{1,0:T(8,128)} %inverse_ref.1), custom_call_target="tpu_custom_call" | custom-call | tf_op jit(solution)/shard_map/pallas_call | solution.py:326
  58.7 4.6 %copy.7 = f32[8,256,512]{2,1,0:T(8,128)} copy(f32[8,256,512]{2,1,0:T(8,128)} %shard_map.55) | data formatting | bytes 8388608
